TPU v7x, 128 devices: a whole 4x4x4 slice. The times are simulated.
128 devices in a mesh: seq: 8 (over x, core), head: 16 (over z, y).
Axes of the slice: x: 4, y: 4, z: 4, core: 2. Of those that a mesh axis runs over, the one named last changes fastest.
Arguments:
- queries: bfloat16 [32768, 2048], P(('seq', 'head')), may hold values from -9 to 9
- keys: bfloat16 [32768, 2048], P(('seq', 'head')), may hold values from -9 to 9
- values: bfloat16 [32768, 2048], P(('seq', 'head')), may hold values from -6 to 6
Outputs:
- attended: bfloat16 [32768, 2048], P(('seq', 'head'))
All inputs are finite; a program needn't handle non-finite values.
Results may differ from a plain program's by a relative error of at most 0.0038.
Values may be sent and summed in bfloat16 or wider, within the bound.
A program may use at most 128 MiB of HBM per device.

v0:
```python
import jax
import jax.numpy as jnp
from jax import lax
from jax.sharding import PartitionSpec as P

HD = 128
SEG = 2048
LEVELS = 5


def attend_rows(query_rows, key_rows, value_rows, query_start):
    factor = query_rows.shape[-1] ** (-0.5)
    scores = (
        jnp.einsum("qd,kd->qk", query_rows, key_rows, preferred_element_type=jnp.float32) * factor
    )
    query_pos = query_start + jnp.arange(query_rows.shape[0], dtype=jnp.int32)
    key_pos = jnp.arange(key_rows.shape[0], dtype=jnp.int32)
    visible = key_pos[None, :] <= query_pos[:, None]
    scores = jnp.where(visible, scores, -jnp.inf)
    row_top = jnp.max(scores, axis=1)
    expo_terms = jnp.exp(scores - row_top[:, None])
    row_total = jnp.sum(expo_terms, axis=1)
    weights = expo_terms.astype(jnp.bfloat16)
    partial_out = jnp.dot(weights, value_rows, preferred_element_type=jnp.float32)
    return (partial_out, row_total, row_top)


def attend_packed(packed):
    return attend_rows(packed[0], packed[1], packed[2], 0)


def dilate(source, seg_rows, stride, offset):
    segments = source.shape[0] // (seg_rows * stride)
    shaped = source.reshape(segments, seg_rows, stride, source.shape[1])
    return lax.dynamic_index_in_dim(shaped, offset, 2, keepdims=False)


def initial_state(length, columns):
    return (
        jnp.full((length,), -jnp.inf, jnp.float32),
        jnp.zeros((length,), jnp.float32),
        jnp.zeros((length, columns), jnp.float32),
    )


def merge_level(carry_state, stride, offset, partial_out, row_total, row_top):
    old_top, old_total, old_acc = carry_state
    length = old_top.shape[0]
    columns = old_acc.shape[1]
    top_view = old_top.reshape(length // stride, stride)
    total_view = old_total.reshape(length // stride, stride)
    acc_view = old_acc.reshape(length // stride, stride, columns)
    top_here = lax.dynamic_index_in_dim(top_view, offset, 1, keepdims=False)
    total_here = lax.dynamic_index_in_dim(total_view, offset, 1, keepdims=False)
    acc_here = lax.dynamic_index_in_dim(acc_view, offset, 1, keepdims=False)
    new_top = jnp.maximum(top_here, row_top)
    keep_old = jnp.exp(top_here - new_top)
    keep_new = jnp.exp(row_top - new_top)
    new_total = total_here * keep_old + row_total * keep_new
    new_acc = acc_here * keep_old[:, None] + partial_out * keep_new[:, None]
    top_view = lax.dynamic_update_index_in_dim(top_view, new_top[:, None], offset, 1)
    total_view = lax.dynamic_update_index_in_dim(total_view, new_total[:, None], offset, 1)
    acc_view = lax.dynamic_update_index_in_dim(acc_view, new_acc[:, None, :], offset, 1)
    return (top_view.reshape(length), total_view.reshape(length), acc_view.reshape(length, columns))


def shards(queries, keys, values):
    q_seq, k_seq, v_seq = (
        lax.all_to_all(queries, "head", split_axis=1, concat_axis=0, tiled=True),
        lax.all_to_all(keys, "head", split_axis=1, concat_axis=0, tiled=True),
        lax.all_to_all(values, "head", split_axis=1, concat_axis=0, tiled=True),
    )
    row_count = q_seq.shape[0]
    head_count = q_seq.shape[1] // HD
    head_base = lax.axis_index("head") * head_count
    seq_index = lax.axis_index("seq")
    remote_levels = lax.axis_size("seq").bit_length() - 1
    local_levels = LEVELS - remote_levels
    k_heads = [k_seq]
    v_heads = [v_seq]

    def own_rows(sources, level_index, seg_rows):
        stride = 2**level_index
        return jnp.stack([dilate(sources[0], seg_rows, stride, (head_base + 0) % stride)[0]])

    remote_keys = []
    for step_index in range(remote_levels):
        level_index = local_levels + step_index
        group_size = SEG * 2**level_index // row_count
        seg_rows = SEG // group_size
        key_part = own_rows(k_heads, level_index, seg_rows)
        value_part = own_rows(v_heads, level_index, seg_rows)
        key_all, value_all = (
            lax.all_gather(key_part, "seq", axis=1, tiled=True),
            lax.all_gather(value_part, "seq", axis=1, tiled=True),
        )
        first_row = (seq_index - seq_index % group_size) * seg_rows
        remote_keys.append(
            (
                lax.dynamic_slice_in_dim(key_all, first_row, SEG, 1),
                lax.dynamic_slice_in_dim(value_all, first_row, SEG, 1),
            )
        )
    states = [initial_state(row_count, HD)]
    for level_index in range(LEVELS):
        stride = 2**level_index
        offset = (head_base + 0) % stride
        if level_index < local_levels:
            query_rows = dilate(q_seq, SEG, stride, offset)
            key_rows = dilate(k_heads[0], SEG, stride, offset)
            value_rows = dilate(v_heads[0], SEG, stride, offset)
            partial_out, row_total, row_top = lax.map(
                attend_packed, (query_rows, key_rows, value_rows)
            )
        else:
            key_full, value_full = remote_keys[level_index - local_levels]
            group_size = SEG * stride // row_count
            seg_rows = SEG // group_size
            query_rows = dilate(q_seq, seg_rows, stride, offset)[0]
            partial_out, row_total, row_top = attend_rows(
                query_rows, key_full[0], value_full[0], seq_index % group_size * seg_rows
            )
        states[0] = merge_level(
            states[0],
            stride,
            offset,
            partial_out.reshape(-1, HD),
            row_total.reshape(-1),
            row_top.reshape(-1),
        )
    head_outputs = [(carry[2] / carry[1][:, None]).astype(jnp.bfloat16) for carry in states]
    joined = head_outputs[0]
    return lax.all_to_all(joined, "head", split_axis=0, concat_axis=1, tiled=True)


def solution(mesh):
    return jax.shard_map(
        shards,
        mesh=mesh,
        in_specs=(P(("seq", "head"), None), P(("seq", "head"), None), P(("seq", "head"), None)),
        out_specs=P(("seq", "head"), None),
        check_vma=False,
    )
```

profile of v0, /device:TPU:0, one launch (start us, length us, event | category | flops | bytes accessed | tf_op | source)
XLA Modules:
  0.0 275.6 jit_solution(6353605494141001700)
XLA Ops:
  6.5 2.2 copy.175
  8.8 8.1 %all-to-all-start.1 = ((bf16[256,16,128]{0,2,1:T(8,128)(2,1)}), bf16[256,16,128]{0,2,1:T(8,128)(2,1)S(1)}, u32[]{:S(2)}, u32[]{:S(2)}) async-start(bf16[256,16,128]{0,2,1:T(8,128)(2,1)} %bitcast.9), calls=%async_computation.1 | async-start | bytes 2097152 | tf_op jit(solution)/shard_map/all_to_all | solution.py:70
  16.9 2.3 copy.173
  19.2 15.4 %all-to-all-done.1 = bf16[256,16,128]{0,2,1:T(8,128)(2,1)S(1)} async-done(((bf16[256,16,128]{0,2,1:T(8,128)(2,1)}), bf16[256,16,128]{0,2,1:T(8,128)(2,1)S(1)}, u32[]{:S(2)}, u32[]{:S(2)}) %all-to-all-start.1) | async-done | bytes 1048608 | tf_op jit(solution)/shard_map/all_to_all | solution.py:70
  34.6 3.7 %all-to-all-start = ((bf16[256,16,128]{0,2,1:T(8,128)(2,1)}), bf16[256,16,128]{0,2,1:T(8,128)(2,1)S(1)}, u32[]{:S(2)}, u32[]{:S(2)}) async-start(bf16[256,16,128]{0,2,1:T(8,128)(2,1)} %bitcast.6), calls=%async_computation | async-start | bytes 2097152 | tf_op jit(solution)/shard_map/all_to_all | solution.py:69
  39.9 2.3 copy.177
  42.2 12.3 %all-to-all-done = bf16[256,16,128]{0,2,1:T(8,128)(2,1)S(1)} async-done(((bf16[256,16,128]{0,2,1:T(8,128)(2,1)}), bf16[256,16,128]{0,2,1:T(8,128)(2,1)S(1)}, u32[]{:S(2)}, u32[]{:S(2)}) %all-to-all-start) | async-done | bytes 1048608 | tf_op jit(solution)/shard_map/all_to_all | solution.py:69
  54.6 4.3 %all-to-all-start.2 = ((bf16[256,16,128]{0,2,1:T(8,128)(2,1)}), bf16[256,16,128]{0,2,1:T(8,128)(2,1)}, u32[]{:S(2)}, u32[]{:S(2)}) async-start(bf16[256,16,128]{0,2,1:T(8,128)(2,1)} %bitcast.12), calls=%async_computation.2 | async-start | bytes 2097152 | tf_op jit(solution)/shard_map/all_to_all | solution.py:71
  60.3 14.3 %all-to-all-done.2 = bf16[256,16,128]{0,2,1:T(8,128)(2,1)} async-done(((bf16[256,16,128]{0,2,1:T(8,128)(2,1)}), bf16[256,16,128]{0,2,1:T(8,128)(2,1)}, u32[]{:S(2)}, u32[]{:S(2)}) %all-to-all-start.2) | async-done | bytes 1048608 | tf_op jit(solution)/shard_map/all_to_all | solution.py:71
  74.7 1.6 copy.178
  76.8 0.7 copy.192
  78.2 19.8 %while.2 = (s32[]{:T(128)}, f32[2,2048,128]{2,1,0:T(8,128)}, f32[2,2048]{1,0:T(2,128)S(1)}, f32[2,2048]{1,0:T(2,128)S(1)}, bf16[2,2048,128]{2,1,0:T(8,128)(2,1)S...) while((s32[]{:T(128)}, f32[2,2048,128]{2,1,0:T(8,128)}, ...), condition=%wide.region_3.4_spmd, body=%wide.region_0.3_spmd.sunk | while | flops 2206199808 | bytes 69798048 | solution.py:112
  78.2 2.4 fusion.116
  80.6 2.6 fusion.117
  83.2 4.7 %fusion.118 = f32[2048]{0:T(1024)S(1)} fusion(f32[2048,2048]{0,1:T(8,128)S(1)} %get-tuple-element.157, f32[2048]{0:T(1024)S(1)} %get-tuple-element.158), kind=kLoop, calls=%fused_computation.3.clone.1 | loop fusion | flops 20969472 | bytes 16793600 | tf_op jit(solution)/shard_map/while/body/eval_jaxpr/reduce_sum | solution.py:22
  88.1 2.4 fusion.116
  90.4 2.6 fusion.117
  93.0 4.7 %fusion.118 = f32[2048]{0:T(1024)S(1)} fusion(f32[2048,2048]{0,1:T(8,128)S(1)} %get-tuple-element.157, f32[2048]{0:T(1024)S(1)} %get-tuple-element.158), kind=kLoop, calls=%fused_computation.3.clone.1 | loop fusion | flops 20969472 | bytes 16793600 | tf_op jit(solution)/shard_map/while/body/eval_jaxpr/reduce_sum | solution.py:22
  97.9 2.0 reshape.199
  99.9 1.6 copy.212
  101.5 1.0 reshape.184
  102.8 1.1 constant_dynamic-slice_fusion.19
  104.0 1.1 constant_dynamic-slice_fusion.20
  105.2 2.4 fusion.24
  107.5 4.8 %fusion.22 = f32[2048]{0:T(1024)S(1)} fusion(f32[2048,2048]{0,1:T(8,128)S(1)} %get-tuple-element.103, f32[2048]{0:T(1024)S(1)} %get-tuple-element.102), kind=kLoop, calls=%fused_computation.23 | loop fusion | flops 20969472 | bytes 16793600 | tf_op jit(solution)/shard_map/while/body/eval_jaxpr/reduce_sum | solution.py:22
  112.4 0.9 copy-done
  113.4 1.3 copy.213
  114.8 2.3 reshape_reshape.36
  117.0 1.3 copy.188
  118.4 4.7 %dynamic_update_slice.66 = f32[2048,2]{1,0:T(8,128)S(1)} dynamic-update-slice(f32[2048,2]{1,0:T(8,128)S(1)} %reshape.184, f32[2048,1]{1,0:T(8,128)} %copy.188, s32[]{:T(128)} %constant.274.clone.1, s32[]{:T(128)S(6)} %select_n.159) | dynamic-update-slice | bytes 16388 | tf_op jit(solution)/shard_map/jit(dynamic_update_index_in_dim)/dynamic_update_slice | solution.py:61
  123.1 1.0 reshape_reshape.31
  124.1 1.5 constant_dynamic-slice_fusion.2
  126.2 1.8 constant_dynamic-slice_fusion.13
  128.0 0.7 copy.194
  128.8 2.2 constant_dynamic-slice_fusion.18
  131.0 3.2 %fusion.50 = f32[2048,2,128]{2,0,1:T(8,128)S(1)} fusion(f32[2048,2,128]{2,1,0:T(2,128)} %bitcast.175, f32[2048,2]{0,1:T(2,128)S(1)} %get-tuple-element.100, f32[2048,2]{0,1:T(2,128)S(1)} %get-tuple-element.101), kind=kLoop, calls=%fused_computation.49 | loop fusion | flops 1048576 | bytes 4227072 | tf_op jit(solution)/shard_map/add | solution.py:60
  134.1 9.1 %fusion.44 = f32[2048,2,128]{2,0,1:T(8,128)S(1)} fusion(f32[2048,2,128]{2,0,1:T(8,128)S(1)} %fusion.50, s32[]{:T(128)S(6)} %select_n.159, f32[2048,2048]{0,1:T(8,128)} %copy-done, f32[2048]{0:T(1024)S(1)} %get-tuple-element.102, bf16[1,2048,1,128]{3,2,1,0:T(2,128)(2,1)S(1)} %constant_dynamic-slice_fusion.18, f32[2048]{0:T(1024)S(1)} %bitcast.194, ...), kind=kOutput, calls=%fused_computation.44 | convolution fusion | flops 1095499776 | bytes 19947524 | tf_op jit(solution)/shard_map/while/body/eval_jaxpr/dot_general | solution.py:24
  143.3 7.6 %copy.187 = f32[2048,2,128]{2,1,0:T(2,128)S(1)} copy(f32[2048,2,128]{2,0,1:T(8,128)S(1)} %fusion.44) | data formatting | bytes 4194304 | tf_op jit(solution)/shard_map/jit(dynamic_update_index_in_dim)/dynamic_update_slice | solution.py:63
  150.9 1.5 constant_dynamic-slice_fusion.8
  153.1 1.2 constant_dynamic-slice_fusion.3
  154.7 1.3 constant_dynamic-slice_fusion.15
  156.0 1.3 constant_dynamic-slice_fusion.17
  157.3 13.4 %all-gather.4 = bf16[1,2048,1,128]{3,1,2,0:T(8,128)(2,1)S(1)} all-gather(bf16[1,256,1,128]{3,1,2,0:T(8,128)(2,1)S(1)} %copy.208), channel_id=6, replica_groups=mesh['seq'=8,'head'=16] {'seq'}, dimensions={1}, use_global_device_ids=true | all-gather | bytes 589824 | tf_op jit(solution)/shard_map/all_gather | solution.py:94
  171.3 1.3 copy-done.3
  173.1 14.4 %all-gather.5 = bf16[1,2048,1,128]{3,1,2,0:T(8,128)(2,1)} all-gather(bf16[1,256,1,128]{3,1,2,0:T(8,128)(2,1)S(1)} %copy.210), channel_id=7, replica_groups=mesh['seq'=8,'head'=16] {'seq'}, dimensions={1}, use_global_device_ids=true | all-gather | bytes 589824 | tf_op jit(solution)/shard_map/all_gather | solution.py:95
  187.5 2.0 fusion.107
  189.5 2.0 copy-done.1
  192.2 5.4 %fusion.29 = (f32[1024]{0:T(1024)S(1)}, f32[1024,2048]{1,0:T(8,128)}) fusion(s32[1024]{0:T(1024)S(1)} %copy-done.10, bf16[1,8192,1,128]{3,1,2,0:T(8,128)(2,1)} %all-gather.11.cloned.1.call-done, s32[]{:T(128)S(6)} %select_n.164, bf16[1,1024,1,128]{3,2,1,0:T(2,128)(2,1)S(1)} %copy-done.9), kind=kOutput, calls=%fused_computation.32 | convolution fusion | flops 545258496 | bytes 9183236 | tf_op jit(solution)/shard_map/qd,kd->qk/dot_general | solution.py:14
  197.7 4.9 %fusion.27 = f32[1024]{0:T(1024)S(1)} fusion(f32[1024,2048]{1,0:T(8,128)} %get-tuple-element.105, f32[1024]{0:T(1024)S(1)} %get-tuple-element.104, s32[1024]{0:T(1024)S(1)} %copy-done.10), kind=kLoop, calls=%fused_computation.30 | loop fusion | flops 10484736 | bytes 8400896 | tf_op jit(solution)/shard_map/reduce_sum | solution.py:22
  202.6 1.0 copy.215
  203.6 2.4 dynamic_update_slice.73
  206.7 2.0 dynamic_update_slice.68
  209.2 0.9 dynamic_update_slice.74
  210.6 0.9 dynamic_update_slice.70
  212.0 0.7 dynamic_update_slice.75
  212.9 5.9 %fusion.57 = f32[1024,128]{1,0:T(8,128)S(1)} fusion(f32[1024,2048]{1,0:T(8,128)} %get-tuple-element.105, f32[1024]{0:T(1024)S(1)} %get-tuple-element.104, s32[1024]{0:T(1024)S(1)} %copy-done.10, bf16[1,8192,1,128]{3,1,2,0:T(8,128)(2,1)} %all-gather.13.cloned.1.call-done, s32[]{:T(128)S(6)} %select_n.164, f32[1024,128]{1,0:T(8,128)} %bitcast.183, ...), kind=kOutput, calls=%fused_computation.56 | convolution fusion | flops 547749888 | bytes 9977860 | tf_op jit(solution)/shard_map/dot_general | solution.py:24
  218.8 11.5 %dynamic_update_slice.67 = f32[1024,4,128]{2,1,0:T(4,128)S(1)} dynamic-update-slice(f32[1024,4,128]{2,1,0:T(4,128)S(1)} %bitcast.150, f32[1024,1,128]{2,1,0:T(1,128)S(1)} %bitcast.182, s32[]{:T(128)} %constant.274.clone.1, s32[]{:T(128)S(6)} %select_n.162, s32[]{:T(128)} %constant.274.clone.1) | dynamic-update-slice | bytes 1048580 | tf_op jit(solution)/shard_map/jit(dynamic_update_index_in_dim)/dynamic_update_slice | solution.py:63
  230.5 3.1 %fusion.63 = f32[512,128]{1,0:T(8,128)S(1)} fusion(f32[512,2048]{1,0:T(8,128)} %copy-done.1, f32[512]{0:T(512)S(1)} %get-tuple-element.106, bf16[1,4096,1,128]{3,1,2,0:T(8,128)(2,1)} %all-gather.17.cloned.1.call-done, s32[]{:T(128)S(6)} %select_n.169, f32[512,128]{1,0:T(8,128)S(1)} %bitcast.176, f32[512]{0:T(512)S(1)} %bitcast.192, f32[512]{0:T(512)S(1)} %bitcast.191), kind=kOutput, calls=%fused_computation.58 | convolution fusion | flops 270729216 | bytes 5249028 | tf_op jit(solution)/shard_map/dot_general | solution.py:24
  233.6 5.6 %dynamic_update_slice.69 = f32[512,8,128]{2,1,0:T(8,128)S(1)} dynamic-update-slice(f32[512,8,128]{2,1,0:T(8,128)S(1)} %bitcast.152, f32[512,1,128]{2,1,0:T(1,128)S(1)} %bitcast.177, s32[]{:T(128)} %constant.274.clone.1, s32[]{:T(128)S(6)} %select_n.167, s32[]{:T(128)} %constant.274.clone.1) | dynamic-update-slice | bytes 524292 | tf_op jit(solution)/shard_map/jit(dynamic_update_index_in_dim)/dynamic_update_slice | solution.py:63
  239.4 2.1 fusion.66
  241.4 2.8 %dynamic_update_slice.71 = f32[256,16,128]{2,1,0:T(8,128)S(1)} dynamic-update-slice(f32[256,16,128]{2,1,0:T(8,128)S(1)} %bitcast.154, f32[256,1,128]{2,1,0:T(1,128)S(1)} %bitcast.180, s32[]{:T(128)} %constant.274.clone.1, s32[]{:T(128)S(6)} %select_n.172, s32[]{:T(128)} %constant.274.clone.1) | dynamic-update-slice | bytes 262148 | tf_op jit(solution)/shard_map/jit(dynamic_update_index_in_dim)/dynamic_update_slice | solution.py:63
  244.3 0.7 fusion.49
  245.0 21.8 %all_to_all.64 = bf16[16,256,128]{2,1,0:T(8,128)(2,1)S(1)} all-to-all(bf16[16,256,128]{2,1,0:T(8,128)(2,1)S(1)} %fusion.49), channel_id=1, replica_groups=mesh['seq'=8,'head'=16] {'head'}, dimensions={0} | all-to-all | bytes 2097152 | tf_op jit(solution)/shard_map/all_to_all | solution.py:133
  267.4 1.4 copy.221
  (88 shorter events, 11.5 us)
Async XLA Ops:
  8.8 25.8 %all-to-all-start.1 = ((bf16[256,16,128]{0,2,1:T(8,128)(2,1)}), bf16[256,16,128]{0,2,1:T(8,128)(2,1)S(1)}, u32[]{:S(2)}, u32[]{:S(2)}) async-start(bf16[256,16,128]{0,2,1:T(8,128)(2,1)} %bitcast.9), calls=%async_computation.1 | async-start | bytes 2097152 | tf_op jit(solution)/shard_map/all_to_all | solution.py:70
  34.6 20.0 %all-to-all-start = ((bf16[256,16,128]{0,2,1:T(8,128)(2,1)}), bf16[256,16,128]{0,2,1:T(8,128)(2,1)S(1)}, u32[]{:S(2)}, u32[]{:S(2)}) async-start(bf16[256,16,128]{0,2,1:T(8,128)(2,1)} %bitcast.6), calls=%async_computation | async-start | bytes 2097152 | tf_op jit(solution)/shard_map/all_to_all | solution.py:69
  38.2 149.3 %all-gather.15.cloned.1.call-start = ((), (), s32[]{:S(2)}) async-start(), calls=%async_computation.6 | async-start | bytes 1179648 | tf_op jit(solution)/shard_map/all_gather | solution.py:94
  54.6 20.1 %all-to-all-start.2 = ((bf16[256,16,128]{0,2,1:T(8,128)(2,1)}), bf16[256,16,128]{0,2,1:T(8,128)(2,1)}, u32[]{:S(2)}, u32[]{:S(2)}) async-start(bf16[256,16,128]{0,2,1:T(8,128)(2,1)} %bitcast.12), calls=%async_computation.2 | async-start | bytes 2097152 | tf_op jit(solution)/shard_map/all_to_all | solution.py:71
  58.9 133.3 %all-gather.11.cloned.1.call-start = ((), (), s32[]{:S(2)}) async-start(), calls=%async_computation.4 | async-start | bytes 2359296 | tf_op jit(solution)/shard_map/all_gather | solution.py:94
  77.6 135.3 %all-gather.13.cloned.1.call-start = ((), (), s32[]{:S(2)}) async-start(), calls=%async_computation.5 | async-start | bytes 2359296 | tf_op jit(solution)/shard_map/all_gather | solution.py:95
  78.2 2.4 copy-start.6
  83.2 4.7 %copy-start.7 = (f32[2,2048,128]{2,1,0:T(8,128)}, f32[2,2048,128]{2,1,0:T(8,128)S(1)}, u32[]{:S(2)}) copy-start(f32[2,2048,128]{2,1,0:T(8,128)S(1)} %fusion.117) | copy-start | bytes 6291460 | tf_op jit(solution)/shard_map/while
  88.1 2.4 copy-start.6
  93.0 4.7 %copy-start.7 = (f32[2,2048,128]{2,1,0:T(8,128)}, f32[2,2048,128]{2,1,0:T(8,128)S(1)}, u32[]{:S(2)}) copy-start(f32[2,2048,128]{2,1,0:T(8,128)S(1)} %fusion.117) | copy-start | bytes 6291460 | tf_op jit(solution)/shard_map/while
  97.9 3.6 %copy-start.2 = (bf16[2,2048,128]{2,1,0:T(8,128)(2,1)}, bf16[2,2048,128]{2,1,0:T(8,128)(2,1)S(1)}, u32[]{:S(2)}) copy-start(bf16[2,2048,128]{2,1,0:T(8,128)(2,1)S(1)} %get-tuple-element.192) | copy-start | bytes 3145732
  107.5 5.7 %copy-start = (f32[2048,2048]{0,1:T(8,128)}, f32[2048,2048]{0,1:T(8,128)S(1)}, u32[]{:S(2)}) copy-start(f32[2048,2048]{0,1:T(8,128)S(1)} %get-tuple-element.103) | copy-start | bytes 50331652
  128.7 101.8 %all-gather.17.cloned.1.call-start = ((), (), s32[]{:S(2)}) async-start(), calls=%async_computation.7 | async-start | bytes 1179648 | tf_op jit(solution)/shard_map/all_gather | solution.py:95
  156.0 36.2 %copy-start.9 = (bf16[1,1024,1,128]{3,2,1,0:T(2,128)(2,1)S(1)}, bf16[1,1024,1,128]{3,2,1,0:T(2,128)(2,1)}, u32[]{:S(2)}) copy-start(bf16[1,1024,1,128]{3,2,1,0:T(2,128)(2,1)} %constant_dynamic-slice_fusion.15) | copy-start | bytes 786436
  156.0 36.2 %copy-start.10 = (s32[1024]{0:T(1024)S(1)}, s32[1024]{0:T(1024)}, u32[]{:S(2)}) copy-start(s32[1024]{0:T(1024)} %iota_add_fusion) | copy-start | bytes 12292
  171.3 1.3 copy-start.3
  189.5 2.0 copy-start.1
  197.7 6.0 %copy-start.5 = (f32[1024,4]{1,0:T(8,128)S(1)}, f32[1024,4]{1,0:T(8,128)}, u32[]{:S(2)}) copy-start(f32[1024,4]{1,0:T(8,128)} %reshape_reshape.36) | copy-start | bytes 49156
  197.7 9.0 %copy-start.4 = (f32[1024,4]{1,0:T(8,128)S(1)}, f32[1024,4]{1,0:T(8,128)}, u32[]{:S(2)}) copy-start(f32[1024,4]{1,0:T(8,128)} %reshape_reshape.31) | copy-start | bytes 49156
  212.8 26.5 %copy-start.8 = (bf16[1,2048,1,128]{3,1,2,0:T(8,128)(2,1)S(1)}, bf16[1,2048,1,128]{3,1,2,0:T(8,128)(2,1)}, u32[]{:S(2)}) copy-start(bf16[1,2048,1,128]{3,1,2,0:T(8,128)(2,1)} %all-gather.5) | copy-start | bytes 1572868
Sparse Core Ops, SparseCore 0:
  40.8 24.7 all-gather.14
  77.7 22.5 all-gather.10
  128.9 22.8 all-gather.12
  187.6 20.1 all-gather.16
where the time goes:
time: 280 us; the launch traced here: 276 us
  local copies, waits for them, and re-layouts  87.4 us (31%)
  blocking collectives  49.7 us (18%)
  waiting for transfers between devices  42.2 us (15%)
  matrix products  40.5 us (14%)
  other arithmetic  24.8 us (9%)
  starting transfers between devices  16.8 us (6%)
  between operations  14.1 us (5%)
    dynamic_update_slice x4, local copies, waits for them, and re-layouts, merge_level(): lax.dynamic_update_index_in_dim(acc_view, new_acc[:, None, :], offset, 1)  27.6 us
    dot_general x6, matrix products, attend_rows(): jnp.dot(weights, value_rows, preferred_element_type=jnp.float32)  25.4 us
    all_to_all x1, blocking collectives, shards(): lax.all_to_all(joined, 'head', split_axis=0, concat_axis=1, tiled=True)  21.8 us
    reduce_sum x6, other arithmetic, attend_rows(): row_total = jnp.sum(expo_terms, axis=1)  20.2 us
    all_to_all x1, waiting for transfers between devices, shards(): lax.all_to_all(keys, 'head', split_axis=1, concat_axis=0, tiled=True)  15.4 us
    dot_general x6, matrix products, attend_rows(): jnp.einsum('qd,kd->qk', query_rows, key_rows, preferred_element_type=jnp....  15.1 us
    dynamic_slice x18, local copies, waits for them, and re-layouts, dilate(): return lax.dynamic_index_in_dim(shaped, offset, 2, keepdims=False)  14.5 us
    all_gather x1, blocking collectives, shards(): lax.all_gather(value_part, 'seq', axis=1, tiled=True)  14.4 us
  transfers between devices with their start and end apart: 7, of which 3 were waited for; matrix products, arithmetic and copies ran while one was open for 47% of the time, Pallas kernels for 0%

commit v1 on v0

v1 whole, which is shorter than its diff:
```python
import functools
import math

import jax
import jax.numpy as jnp
from jax import lax
from jax.experimental import pallas as pl
from jax.experimental.pallas import tpu as pltpu
from jax.sharding import PartitionSpec as P

HD = 128
BLK = 256
NB = 16
CH = 64
NCH = BLK // CH
SCALE = HD**-0.5 * math.log2(math.e)
LOW = -1e30
MESH = pl.DeviceIdType.MESH

ORDER = [
    (0, 1), (0, 3), (1, 0), (3, 0),
    (1, 1), (3, 3), (1, 3), (3, 1),
    (2, 2), (0, 2), (2, 0),
    (1, 2), (3, 2), (2, 1), (2, 3),
]

KV_PARTS = [(0, 64), (64, 128), (128, 256)]
Q_PARTS = [(i * CH, (i + 1) * CH) for i in range(NCH)]


def token_of(row, head):
    group = row // 16
    shift = jnp.where(
        group >= 8,
        1 + (group - 8) * 2,
        jnp.where(
            group >= 4,
            2 + (group - 4) * 4,
            jnp.where(group >= 2, 4 + (group - 2) * 8, jnp.where(group >= 1, 8, 0)),
        ),
    )
    return (row % 16) * 16 + (shift + head) % 16


def class_of(row):
    return (
        (row < 128).astype(jnp.int32)
        + (row < 64).astype(jnp.int32)
        + (row < 32).astype(jnp.int32)
        + (row < 16).astype(jnp.int32)
    )


def iota(shape, dim):
    return lax.broadcasted_iota(jnp.int32, shape, dim)


def kernel(
    q_hbm, k_hbm, v_hbm, out_ref,
    x_in, q_send, k_send, v_send, q_recv, k_recv, v_recv, o_send, o_recv,
    kx2, vx2, kx3, vx3, kx4, vx4,
    m_ref, acc_ref, bias_ref, mult0, mult1, mult2, mult3,
    in_sem, q_ss, k_ss, v_ss, o_ss, q_rs, k_rs, v_rs, o_rs, x_ss, x_rs,
):
    seq = lax.axis_index("seq")
    me = lax.axis_index("head")
    z, y = me // 4, me % 4
    flip = 1 + 2 * (seq % 2)
    peers = [((z + dz * flip) % 4) * 4 + (y + dy * flip) % 4 for dz, dy in ORDER]

    loads = []
    for i, src in enumerate((k_hbm, v_hbm, q_hbm)):
        cp = pltpu.make_async_copy(src, x_in.at[i], in_sem.at[i])
        cp.start()
        loads.append(cp)

    barrier = pltpu.get_barrier_semaphore()
    for p in peers:
        pl.semaphore_signal(barrier, inc=1, device_id=(seq, p), device_id_type=MESH)
    for d in range(1, 8):
        pl.semaphore_signal(
            barrier, inc=1, device_id=((seq + d) % 8, me), device_id_type=MESH
        )

    def sort_rows(i, dst):
        def body(j, carry):
            tok = token_of(iota((BLK, BLK), 0), j)
            perm = (iota((BLK, BLK), 1) == tok).astype(jnp.bfloat16)
            cols = x_in[i, :, pl.ds(pl.multiple_of(j * HD, HD), HD)]
            dst[j] = jnp.dot(perm, cols, preferred_element_type=jnp.float32).astype(
                jnp.bfloat16
            )
            return carry

        lax.fori_loop(0, NB, body, 0)

    def send(src, dst, ssem, rsem, part, idx):
        lo, hi = part
        rows = pl.ds(lo, hi - lo)
        for p in peers:
            pltpu.make_async_remote_copy(
                src_ref=src.at[p, rows],
                dst_ref=dst.at[me, rows],
                send_sem=ssem.at[idx],
                recv_sem=rsem.at[idx],
                device_id=(seq, p),
                device_id_type=MESH,
            ).start()

    def wait_all(buf, sem, part, idx):
        lo, hi = part
        view = buf.at[pl.ds(0, NB - 1), pl.ds(lo, hi - lo)]
        pltpu.make_async_copy(view, view, sem.at[idx]).wait()

    loads[0].wait()
    sort_rows(0, k_send)
    k_recv[me] = k_send[me]
    pl.semaphore_wait(barrier, NB - 1 + 7)
    send(k_send, k_recv, k_ss, k_rs, KV_PARTS[0], 0)
    loads[1].wait()
    sort_rows(1, v_send)
    v_recv[me] = v_send[me]
    send(v_send, v_recv, v_ss, v_rs, KV_PARTS[0], 0)
    loads[2].wait()
    sort_rows(2, q_send)
    q_recv[me] = q_send[me]
    send(q_send, q_recv, q_ss, q_rs, Q_PARTS[0], 0)
    for i in range(1, len(KV_PARTS)):
        send(k_send, k_recv, k_ss, k_rs, KV_PARTS[i], i)
        send(v_send, v_recv, v_ss, v_rs, KV_PARTS[i], i)
    for i in range(1, NCH):
        send(q_send, q_recv, q_ss, q_rs, Q_PARTS[i], i)

    row_tok = token_of(iota((BLK, BLK), 0), me)
    col_tok = token_of(iota((BLK, BLK), 1), me)
    bias_ref[...] = jnp.where(col_tok <= row_tok, 0.0, LOW)
    for ref, period, level in ((mult0, 128, 0), (mult1, 128, 1), (mult2, 64, 2), (mult3, 32, 3)):
        shape = ref.shape
        both = jnp.minimum(
            class_of(iota(shape, 0)), class_of(iota(shape, 1) % period)
        )
        ref[...] = (1 + both - level).astype(jnp.float32)
    m_ref[...] = jnp.full(m_ref.shape, LOW, jnp.float32)
    acc_ref[...] = jnp.zeros(acc_ref.shape, jnp.float32)

    wait_all(k_recv, k_rs, KV_PARTS[0], 0)
    wait_all(v_recv, v_rs, KV_PARTS[0], 0)

    def hop(src, dst, idx, target):
        return pltpu.make_async_remote_copy(
            src_ref=src,
            dst_ref=dst,
            send_sem=x_ss.at[idx],
            recv_sem=x_rs.at[idx],
            device_id=(target, me),
            device_id_type=MESH,
        )

    @pl.when(seq < 4)
    def _():
        for t in range(4, 8):
            hop(k_recv.at[:, pl.ds(0, 16)], kx4.at[seq % 4], 4, t).start()
            hop(v_recv.at[:, pl.ds(0, 16)], vx4.at[seq % 4], 5, t).start()

    @pl.when(seq % 4 < 2)
    def _():
        for t in range(2, 4):
            hop(k_recv.at[:, pl.ds(0, 32)], kx3.at[seq % 2], 2, (seq // 4) * 4 + t).start()
            hop(v_recv.at[:, pl.ds(0, 32)], vx3.at[seq % 2], 3, (seq // 4) * 4 + t).start()

    @pl.when(seq % 2 == 0)
    def _():
        hop(k_recv.at[:, pl.ds(0, 64)], kx2, 0, (seq // 2) * 2 + 1).start()
        hop(v_recv.at[:, pl.ds(0, 64)], vx2, 1, (seq // 2) * 2 + 1).start()

    def flash(chunk, blk0, nblk, rows, keys, vals, mask=False, mults=(), first=False):
        lo, hi = rows
        height = hi - lo
        length = nblk * height
        blocks = pl.ds(blk0, nblk)
        q = q_recv[blocks, pl.ds(chunk * CH + lo, height)].reshape(length, HD)
        s = lax.dot_general(
            q, keys, (((1,), (1,)), ((), ())), preferred_element_type=jnp.float32
        )
        if mask:
            s0 = s[:height] + bias_ref[pl.ds(chunk * CH + lo, height)]
            s = s0 if nblk == 1 else jnp.concatenate([s0, s[height:]], axis=0)
        width = keys.shape[0]
        lanes = [s[:, i : i + HD] for i in range(0, width, HD)]
        top = functools.reduce(jnp.maximum, lanes)
        top = jnp.broadcast_to(jnp.max(top, axis=1, keepdims=True), (length, HD))
        here = pl.ds(lo, height)
        if not first:
            old = m_ref[blocks, here].reshape(length, HD)
            top = jnp.maximum(old, top)
            keep = jnp.exp2((old - top) * SCALE)
        m_ref[blocks, here] = top.reshape(nblk, height, HD)
        weights = []
        for i, part in enumerate(lanes):
            w = jnp.exp2((part - top) * SCALE)
            if i < len(mults) and mults[i] is not None:
                w = (w.reshape(nblk, height, HD) * mults[i][None]).reshape(length, HD)
            weights.append(w.astype(jnp.bfloat16))
        w = jnp.concatenate(weights, axis=1)
        ones = jnp.ones((width, HD), jnp.bfloat16)
        pv = jnp.dot(
            w, jnp.concatenate([vals, ones], axis=1), preferred_element_type=jnp.float32
        )
        if not first:
            old_acc = acc_ref[blocks, here].reshape(length, 2 * HD)
            pv = pv + old_acc * jnp.concatenate([keep, keep], axis=1)
        acc_ref[blocks, here] = pv.reshape(nblk, height, 2 * HD)

    def cross(chunk, blk0, nblk, rows, key_at, val_at, mult):
        def body(j, carry):
            flash(chunk, blk0, nblk, rows, key_at(j), val_at(j), mults=[mult] * 4)
            return carry

        lax.fori_loop(0, 2, body, 0)

    wait_all(q_recv, q_rs, Q_PARTS[0], 0)

    @pl.when(seq % 2 == 1)
    def _():
        hop(kx2, kx2, 0, seq).wait_recv()
        hop(vx2, vx2, 1, seq).wait_recv()
        for g in range(2):
            cross(
                0, g * 8, 8, (0, 64),
                lambda j: kx2[pl.ds(j * 8, 8)].reshape(512, HD),
                lambda j: vx2[pl.ds(j * 8, 8)].reshape(512, HD),
                mult2[...],
            )

    @pl.when(seq % 4 >= 2)
    def _():
        hop(kx3, kx3, 2, seq).wait_recv()
        hop(vx3, vx3, 3, seq).wait_recv()
        cross(
            0, 0, NB, (0, 32),
            lambda j: kx3[j].reshape(512, HD),
            lambda j: vx3[j].reshape(512, HD),
            mult3[...],
        )

    @pl.when(seq >= 4)
    def _():
        hop(kx4, kx4, 4, seq).wait_recv()
        hop(vx4, vx4, 5, seq).wait_recv()
        cross(
            0, 0, NB, (0, 16),
            lambda j: kx4[pl.ds(j * 2, 2)].reshape(512, HD),
            lambda j: vx4[pl.ds(j * 2, 2)].reshape(512, HD),
            None,
        )

    for i in range(1, len(KV_PARTS)):
        wait_all(k_recv, k_rs, KV_PARTS[i], i)
        wait_all(v_recv, v_rs, KV_PARTS[i], i)

    for chunk in range(NCH):
        if chunk > 0:
            wait_all(q_recv, q_rs, Q_PARTS[chunk], chunk)
        lo = chunk * CH
        nested = lo < 128

        def segment(g, carry, chunk=chunk, lo=lo, nested=nested):
            for kb in range(8):
                flash(
                    chunk, g * 8 + kb, 8 - kb, (0, CH),
                    k_recv[g * 8 + kb], v_recv[g * 8 + kb],
                    mask=True,
                    mults=[mult0[pl.ds(lo, CH)]] if nested else (),
                    first=chunk > 0 and kb == 0,
                )
            return carry

        lax.fori_loop(0, 2, segment, 0)
        if nested:
            cross(
                chunk, 8, 8, (0, CH),
                lambda j: k_recv[pl.ds(j * 4, 4), pl.ds(0, 128)].reshape(512, HD),
                lambda j: v_recv[pl.ds(j * 4, 4), pl.ds(0, 128)].reshape(512, HD),
                mult1[...] if chunk == 0 else None,
            )
        for b in range(NB):
            acc = acc_ref[b]
            o_send[b, pl.ds(lo, CH)] = (acc[:, :HD] / acc[:, HD:]).astype(jnp.bfloat16)
        o_recv[me, pl.ds(lo, CH)] = o_send[me, pl.ds(lo, CH)]
        send(o_send, o_recv, o_ss, o_rs, Q_PARTS[chunk], chunk)

    for i in range(NCH):
        wait_all(o_recv, o_rs, Q_PARTS[i], i)

    def unsort(j, carry):
        tok = token_of(iota((BLK, BLK), 1), j)
        perm = (iota((BLK, BLK), 0) == tok).astype(jnp.bfloat16)
        out_ref[:, pl.ds(pl.multiple_of(j * HD, HD), HD)] = jnp.dot(
            perm, o_recv[j], preferred_element_type=jnp.float32
        ).astype(jnp.bfloat16)
        return carry

    lax.fori_loop(0, NB, unsort, 0)

    for i, part in enumerate(KV_PARTS):
        wait_all(k_send, k_ss, part, i)
        wait_all(v_send, v_ss, part, i)
    for i, part in enumerate(Q_PARTS):
        wait_all(q_send, q_ss, part, i)
        wait_all(o_send, o_ss, part, i)

    @pl.when(seq < 4)
    def _():
        hop(kx4, kx4, 4, seq).wait_send()
        hop(vx4, vx4, 5, seq).wait_send()

    @pl.when(seq % 4 < 2)
    def _():
        hop(kx3, kx3, 2, seq).wait_send()
        hop(vx3, vx3, 3, seq).wait_send()

    @pl.when(seq % 2 == 0)
    def _():
        hop(kx2, kx2, 0, seq).wait_send()
        hop(vx2, vx2, 1, seq).wait_send()


def shards(queries, keys, values):
    bf, f32 = jnp.bfloat16, jnp.float32
    vm = pltpu.VMEM
    blocks = vm((NB, BLK, HD), bf)
    dma = pltpu.SemaphoreType.DMA
    nkv = len(KV_PARTS)
    return pl.pallas_call(
        kernel,
        out_shape=jax.ShapeDtypeStruct((BLK, NB * HD), bf),
        in_specs=[pl.BlockSpec(memory_space=pl.ANY)] * 3,
        out_specs=pl.BlockSpec(memory_space=pltpu.VMEM),
        scratch_shapes=[
            vm((3, BLK, NB * HD), bf),
            *[blocks] * 8,
            vm((NB, 64, HD), bf), vm((NB, 64, HD), bf),
            vm((2, NB, 32, HD), bf), vm((2, NB, 32, HD), bf),
            vm((4, NB, 16, HD), bf), vm((4, NB, 16, HD), bf),
            vm((NB, CH, HD), f32), vm((NB, CH, 2 * HD), f32),
            vm((BLK, BLK), f32), vm((128, 128), f32), vm((64, 128), f32),
            vm((64, 128), f32), vm((32, 128), f32),
            dma((3,)), dma((NCH,)), dma((nkv,)), dma((nkv,)), dma((NCH,)),
            dma((NCH,)), dma((nkv,)), dma((nkv,)), dma((NCH,)), dma((6,)), dma((6,)),
        ],
        compiler_params=pltpu.CompilerParams(
            collective_id=0, has_side_effects=True, vmem_limit_bytes=56 * 2**20
        ),
    )(queries, keys, values)


def solution(mesh):
    spec = P(("seq", "head"), None)
    return jax.shard_map(
        shards, mesh=mesh, in_specs=(spec, spec, spec), out_specs=spec, check_vma=False
    )
```

time: 280 us -> 65.4 us (0.23); the launches traced: 276 us -> 65.1 us
  local copies, waits for them, and re-layouts: 87.4 us -> 2.3 us
  Pallas kernels: 0 us -> 62.7 us
  blocking collectives: 49.7 us -> 0 us
  waiting for transfers between devices: 42.2 us -> 0 us
  matrix products: 40.5 us -> 0 us
  other arithmetic: 24.8 us -> 0 us
  starting transfers between devices: 16.8 us -> 0 us
  between operations: 14.1 us -> 0.01 us
    pallas_call x0 -> x1, Pallas kernels: none -> 62.7 us  [shards(): pl.pallas_call(kernel, out_shape=jax.ShapeDtypeStruct((BLK, NB * HD), bf)...]
    all_to_all x3 -> x0, waiting for transfers between devices: 42 us -> none  [the longest x1 15.4 us: shards(): lax.all_to_all(keys, 'head', split_axis=1, concat_axis=0, tiled=True)]
    dynamic_update_slice x16 -> x0, local copies, waits for them, and re-layouts: 41 us -> none  [the longest x4 27.6 us: merge_level(): lax.dynamic_update_index_in_dim(acc_view, new_acc[:, None, :], offset, 1)]
    dot_general x12 -> x0, matrix products: 40.5 us -> none  [the longest x6 25.4 us: attend_rows(): jnp.dot(weights, value_rows, preferred_element_type=jnp.float32)]
    all_gather x2 -> x0, blocking collectives: 27.8 us -> none  [the longest x1 14.4 us: shards(): lax.all_gather(value_part, 'seq', axis=1, tiled=True)]
    all_to_all x1 -> x0, blocking collectives: 21.8 us -> none  [shards(): lax.all_to_all(joined, 'head', split_axis=0, concat_axis=1, tiled=True)]
    reduce_sum x6 -> x0, other arithmetic: 20.2 us -> none  [attend_rows(): row_total = jnp.sum(expo_terms, axis=1)]
    dynamic_slice x26 -> x0, local copies, waits for them, and re-layouts: 18 us -> none  [the longest x18 14.5 us: dilate(): return lax.dynamic_index_in_dim(shaped, offset, 2, keepdims=False)]
  transfers between devices with their start and end apart: 7 -> 0, of which waited for: 3 -> 0; matrix products, arithmetic and copies ran while one was open for 47% -> 0% of each run, Pallas kernels for 0% -> 0%
where the time goes in v1:
time: 65.4 us; the launch traced here: 65.1 us
  Pallas kernels  62.7 us (96%)
  local copies, waits for them, and re-layouts  2.3 us (4%)
    pallas_call x1, Pallas kernels, shards(): pl.pallas_call(kernel, out_shape=jax.ShapeDtypeStruct((BLK, NB * HD), bf)...  62.7 us
    unnamed x1, local copies, waits for them, and re-layouts  2.3 us

profile of v1, /device:TPU:0, one launch (start us, length us, event | category | flops | bytes accessed | tf_op | source)
XLA Modules:
  0.0 65.1 jit_solution(4024936949223351890)
XLA Ops:
  0.0 62.7 %shard_map.37 = bf16[256,2048]{1,0:T(8,128)(2,1)} custom-call(bf16[256,2048]{1,0:T(8,128)(2,1)} %q_hbm.1, bf16[256,2048]{1,0:T(8,128)(2,1)} %k_hbm.1, bf16[256,2048]{1,0:T(8,128)(2,1)} %v_hbm.1), custom_call_target="tpu_custom_call" | custom-call | tf_op jit(solution)/shard_map/pallas_call | solution.py:334
  62.7 2.3 %copy.5 = bf16[256,2048]{1,0:T(8,128)(2,1)} copy(bf16[256,2048]{1,0:T(8,128)(2,1)} %shard_map.37) | data formatting | bytes 2097152

commit v2 on v1

v2 whole, which is shorter than its diff:
```python
import functools
import math

import jax
import jax.numpy as jnp
from jax import lax
from jax.experimental import pallas as pl
from jax.experimental.pallas import tpu as pltpu
from jax.sharding import PartitionSpec as P

HD = 128
BLK = 256
NB = 16
CH = 64
NCH = BLK // CH
FAR_AFTER = 2
SCALE = HD**-0.5 * math.log2(math.e)
LOW = -1e30
MESH = pl.DeviceIdType.MESH

ORDER = [
    (1, 2), (3, 2), (2, 1), (2, 3),
    (0, 1), (0, 3), (1, 0), (3, 0),
    (2, 2), (1, 1), (3, 3),
    (0, 2), (2, 0), (1, 3), (3, 1),
]

K_PARTS = [(0, 64), (64, 256)]
Q_PARTS = [(i * CH, (i + 1) * CH) for i in range(NCH)]


SHIFTS = [0, 8, 4, 12, 2, 6, 10, 14, 1, 3, 5, 7, 9, 11, 13, 15]


def token_of(row, head):
    group = row >> 4
    shift = jnp.where(
        group >= 8,
        1 + ((group - 8) << 1),
        jnp.where(
            group >= 4,
            2 + ((group - 4) << 2),
            jnp.where(group >= 2, 4 + ((group - 2) << 3), jnp.where(group >= 1, 8, 0)),
        ),
    )
    return ((row & 15) << 4) + ((shift + head) & 15)


def class_of(row):
    return (
        (row < 128).astype(jnp.int32)
        + (row < 64).astype(jnp.int32)
        + (row < 32).astype(jnp.int32)
        + (row < 16).astype(jnp.int32)
    )


def iota(shape, dim):
    return lax.broadcasted_iota(jnp.int32, shape, dim)


def kernel(
    q_hbm, k_hbm, v_hbm, o_recv,
    x_in, q_send, k_send, v_raw, q_recv, k_recv, v_recv, o_send,
    kx2, vx2, kx3, vx3, kx4, vx4,
    m_ref, l_ref, acc_ref, perm_ref, own_perm, bias_ref, mult0, mult1, mult2, mult3,
    in_sem, own_sem, q_ss, k_ss, v_ss, o_ss, q_rs, k_rs, v_rs, o_rs, x_ss, x_rs,
):
    seq = lax.axis_index("seq")
    me = lax.axis_index("head")
    z, y = me // 4, me % 4
    flip = 1 + 2 * (seq % 2)
    peers = [((z + dz * flip) % 4) * 4 + (y + dy * flip) % 4 for dz, dy in ORDER]

    loads = []
    for i, src in enumerate((k_hbm, q_hbm)):
        cp = pltpu.make_async_copy(src, x_in.at[i], in_sem.at[i])
        cp.start()
        loads.append(cp)

    barrier = pltpu.get_barrier_semaphore()
    for p in peers:
        pl.semaphore_signal(barrier, inc=1, device_id=(seq, p), device_id_type=MESH)
    for d in range(1, 8):
        pl.semaphore_signal(
            barrier, inc=1, device_id=((seq + d) % 8, me), device_id_type=MESH
        )

    rows = iota((BLK, BLK), 0)
    perm_ref[...] = (iota((BLK, BLK), 1) == ((rows & 15) << 4) + (rows >> 4)).astype(
        jnp.bfloat16
    )

    def sort_rows(i, dst):
        for j in range(0, NB, 2):
            pair = jnp.dot(
                perm_ref[...],
                x_in[i, :, j * HD : (j + 2) * HD],
                preferred_element_type=jnp.float32,
            ).astype(jnp.bfloat16)
            for h in (j, j + 1):
                cols = pair[:, (h - j) * HD : (h - j + 1) * HD]
                for g, shift in enumerate(SHIFTS):
                    r = (h + shift) % 16
                    dst[h, g * 16 : (g + 1) * 16] = cols[r * 16 : (r + 1) * 16]

    def send(src, dst, ssem, rsem, part, idx, between=()):
        lo, hi = part
        rows = pl.ds(lo, hi - lo)
        for i, p in enumerate(peers):
            pltpu.make_async_remote_copy(
                src_ref=src.at[p, rows],
                dst_ref=dst.at[me, rows],
                send_sem=ssem.at[idx],
                recv_sem=rsem.at[idx],
                device_id=(seq, p),
                device_id_type=MESH,
            ).start()
            if i < len(between):
                between[i]()

    def wait_all(buf, sem, part, idx):
        lo, hi = part
        view = buf.at[pl.ds(0, NB - 1), pl.ds(lo, hi - lo)]
        pltpu.make_async_copy(view, view, sem.at[idx]).wait()

    def head_cols(ref, h):
        return ref.at[:, pl.ds(pl.multiple_of(h * HD, HD), HD)]

    own = pltpu.make_async_copy(head_cols(v_hbm, me), v_raw.at[me], own_sem)
    own.start()
    pl.semaphore_wait(barrier, NB - 1 + 7)
    for p in peers:
        pltpu.make_async_remote_copy(
            src_ref=head_cols(v_hbm, p),
            dst_ref=v_raw.at[me],
            send_sem=v_ss,
            recv_sem=v_rs,
            device_id=(seq, p),
            device_id_type=MESH,
        ).start()
    loads[0].wait()
    sort_rows(0, k_send)
    send(k_send, k_recv, k_ss, k_rs, K_PARTS[0], 0)
    loads[1].wait()
    sort_rows(1, q_send)
    send(q_send, q_recv, q_ss, q_rs, Q_PARTS[0], 0)
    send(k_send, k_recv, k_ss, k_rs, K_PARTS[1], 1)
    k_recv[me] = k_send[me]
    q_recv[me] = q_send[me]

    row_tok = token_of(iota((BLK, BLK), 0), me)
    col_tok = token_of(iota((BLK, BLK), 1), me)
    own_perm[...] = (iota((BLK, BLK), 1) == row_tok).astype(jnp.bfloat16)
    bias_ref[...] = jnp.where(col_tok <= row_tok, 0.0, LOW)
    for ref, period, level in ((mult0, 128, 0), (mult1, 128, 1), (mult2, 64, 2), (mult3, 32, 3)):
        shape = ref.shape
        both = jnp.minimum(
            class_of(iota(shape, 0)), class_of(iota(shape, 1) & (period - 1))
        )
        ref[...] = (1 + both - level).astype(jnp.float32)

    m_ref[0] = jnp.full(m_ref.shape[1:], LOW, jnp.float32)
    l_ref[0] = jnp.zeros(l_ref.shape[1:], jnp.float32)
    acc_ref[0] = jnp.zeros(acc_ref.shape[1:], jnp.float32)

    own.wait()
    arrived = v_raw.at[pl.ds(0, NB - 1)]
    pltpu.make_async_copy(arrived, arrived, v_rs).wait()
    for b in range(0, NB, 2):
        pair = jnp.dot(
            own_perm[...],
            jnp.concatenate([v_raw[b], v_raw[b + 1]], axis=1),
            preferred_element_type=jnp.float32,
        ).astype(jnp.bfloat16)
        v_recv[b] = pair[:, :HD]
        v_recv[b + 1] = pair[:, HD:]
    wait_all(k_recv, k_rs, K_PARTS[0], 0)

    def hop(src, dst, idx, target):
        return pltpu.make_async_remote_copy(
            src_ref=src,
            dst_ref=dst,
            send_sem=x_ss.at[idx],
            recv_sem=x_rs.at[idx],
            device_id=(target, me),
            device_id_type=MESH,
        )

    @pl.when(seq % 2 == 0)
    def _():
        hop(k_recv.at[:, pl.ds(0, 64)], kx2, 0, (seq // 2) * 2 + 1).start()
        hop(v_recv.at[:, pl.ds(0, 64)], vx2, 1, (seq // 2) * 2 + 1).start()

    core = seq % 2
    partner = seq + 1 - 2 * core
    near_chip = seq % 4 < 2
    far_chip = seq < 4

    def hop3(src, dst, idx):
        @pl.when(near_chip)
        def _():
            hop(src.at[:, pl.ds(0, 32)], dst.at[core], idx, (seq + 2) % 8).start()

    def hop4(src, dst, idx, step):
        @pl.when(far_chip)
        def _():
            target = 4 + 2 * step + core
            hop(src.at[:, pl.ds(0, 16)], dst.at[core, seq // 2 % 2], idx, target).start()

    hops = [functools.partial(hop3, *x) for x in ((k_recv, kx3, 2), (v_recv, vx3, 3))]
    hops += [
        functools.partial(hop4, *x, step)
        for step in range(2)
        for x in ((k_recv, kx4, 4), (v_recv, vx4, 5))
    ]
    send(q_send, q_recv, q_ss, q_rs, Q_PARTS[1], 1, between=hops)
    for i in range(2, NCH):
        send(q_send, q_recv, q_ss, q_rs, Q_PARTS[i], i)

    def hand_over():
        for here, pairs in (
            (jnp.logical_not(near_chip), ((kx3, 2), (vx3, 3))),
            (jnp.logical_not(far_chip), ((kx4, 4), (vx4, 5))),
        ):

            @pl.when(here)
            def _(pairs=pairs):
                for buf, idx in pairs:
                    hop(buf.at[core], buf.at[core], idx, partner).wait_recv()
                    hop(buf.at[core], buf.at[core], idx + 4, partner).start()

    def flash(chunk, blk0, nblk, rows, keys, vals, mask=False, mults=(), first=False):
        lo, hi = rows
        height = hi - lo
        length = nblk * height
        blocks = pl.ds(blk0, nblk)
        q = q_recv[blocks, pl.ds(chunk * CH + lo, height)].reshape(length, HD)
        s = lax.dot_general(
            q, keys, (((1,), (1,)), ((), ())), preferred_element_type=jnp.float32
        )
        if mask:
            s0 = s[:height] + bias_ref[pl.ds(chunk * CH + lo, height)]
            s = s0 if nblk == 1 else jnp.concatenate([s0, s[height:]], axis=0)
        width = keys.shape[0]
        lanes = [s[:, i : i + HD] for i in range(0, width, HD)]
        top = functools.reduce(jnp.maximum, lanes)
        top = jnp.broadcast_to(jnp.max(top, axis=1, keepdims=True), (length, HD))
        here = pl.ds(lo, height)
        state = min(chunk, 1)
        if not first:
            old = m_ref[state, blocks, here].reshape(length, HD)
            top = jnp.maximum(old, top)
            keep = jnp.exp2((old - top) * SCALE)
        m_ref[state, blocks, here] = top.reshape(nblk, height, HD)
        weights = []
        total = jnp.zeros((length, HD), jnp.float32)
        for i, part in enumerate(lanes):
            w = jnp.exp2((part - top) * SCALE)
            if i < len(mults) and mults[i] is not None:
                w = (w.reshape(nblk, height, HD) * mults[i][None]).reshape(length, HD)
            total = total + w
            weights.append(w.astype(jnp.bfloat16))
        pv = jnp.dot(
            jnp.concatenate(weights, axis=1), vals, preferred_element_type=jnp.float32
        )
        if not first:
            pv = pv + acc_ref[state, blocks, here].reshape(length, HD) * keep
            total = total + l_ref[state, blocks, here].reshape(length, HD) * keep
        acc_ref[state, blocks, here] = pv.reshape(nblk, height, HD)
        l_ref[state, blocks, here] = total.reshape(nblk, height, HD)

    def cross(chunk, blk0, nblk, rows, key_at, val_at, mult):
        for j in range(2):
            flash(chunk, blk0, nblk, rows, key_at(j), val_at(j), mults=[mult] * 4)

    wait_all(q_recv, q_rs, Q_PARTS[0], 0)

    @pl.when(seq % 2 == 1)
    def _():
        hop(kx2, kx2, 0, seq).wait_recv()
        hop(vx2, vx2, 1, seq).wait_recv()
        for g in range(2):
            cross(
                0, g * 8, 8, (0, 64),
                lambda j: kx2[pl.ds(j * 8, 8)].reshape(512, HD),
                lambda j: vx2[pl.ds(j * 8, 8)].reshape(512, HD),
                mult2[...],
            )

    def far_rows():
        @pl.when(seq % 4 >= 2)
        def _():
            hop(kx3.at[1 - core], kx3.at[1 - core], 6, partner).wait_recv()
            hop(vx3.at[1 - core], vx3.at[1 - core], 7, partner).wait_recv()
            cross(
                0, 0, NB, (0, 32),
                lambda j: kx3[j].reshape(512, HD),
                lambda j: vx3[j].reshape(512, HD),
                mult3[...],
            )

        @pl.when(seq >= 4)
        def _():
            hop(kx4.at[1 - core], kx4.at[1 - core], 8, partner).wait_recv()
            hop(vx4.at[1 - core], vx4.at[1 - core], 9, partner).wait_recv()
            cross(
                0, 0, NB, (0, 16),
                lambda j: kx4[j].reshape(512, HD),
                lambda j: vx4[j].reshape(512, HD),
                None,
            )

    wait_all(k_recv, k_rs, K_PARTS[1], 1)

    def own_rows(chunk):
        lo = chunk * CH
        nested = lo < 128

        def segment(g, carry):
            for kb in range(8):
                flash(
                    chunk, g * 8 + kb, 8 - kb, (0, CH),
                    k_recv[g * 8 + kb], v_recv[g * 8 + kb],
                    mask=True,
                    mults=[mult0[pl.ds(lo, CH)]] if nested else (),
                    first=chunk > 0 and kb == 0,
                )
            return carry

        segment(0, 0)
        segment(1, 0)
        if nested:
            cross(
                chunk, 8, 8, (0, CH),
                lambda j: k_recv[pl.ds(j * 4, 4), pl.ds(0, 128)].reshape(512, HD),
                lambda j: v_recv[pl.ds(j * 4, 4), pl.ds(0, 128)].reshape(512, HD),
                mult1[...] if chunk == 0 else None,
            )

    def finish(chunk):
        lo = chunk * CH
        state = min(chunk, 1)
        for b in range(NB):
            total = jnp.sum(l_ref[state, b], axis=1, keepdims=True)
            o_send[b, pl.ds(lo, CH)] = (acc_ref[state, b] / total).astype(jnp.bfloat16)
        o_recv[me, pl.ds(lo, CH)] = o_send[me, pl.ds(lo, CH)]
        send(o_send, o_recv, o_ss, o_rs, Q_PARTS[chunk], chunk)

    own_rows(0)
    for chunk in range(1, NCH):
        wait_all(q_recv, q_rs, Q_PARTS[chunk], chunk)
        own_rows(chunk)
        finish(chunk)
        if chunk == 1:
            hand_over()
        if chunk == FAR_AFTER:
            far_rows()
            finish(0)

    for i in range(NCH):
        wait_all(o_recv, o_rs, Q_PARTS[i], i)

    pltpu.make_async_copy(arrived, arrived, v_ss).wait()
    for i, part in enumerate(K_PARTS):
        wait_all(k_send, k_ss, part, i)
    for i, part in enumerate(Q_PARTS):
        wait_all(q_send, q_ss, part, i)
        wait_all(o_send, o_ss, part, i)

    for first, here, bufs in (
        (2, near_chip, (kx3.at[0], vx3.at[0])),
        (6, jnp.logical_not(near_chip), (kx3.at[0], vx3.at[0])),
        (4, far_chip, (kx4.at[0], vx4.at[0])),
        (8, jnp.logical_not(far_chip), (kx4.at[0], vx4.at[0])),
    ):

        @pl.when(here)
        def _(first=first, bufs=bufs):
            for i, buf in enumerate(bufs):
                hop(buf, buf, first + i, partner).wait_send()

    @pl.when(seq % 2 == 0)
    def _():
        hop(kx2, kx2, 0, seq).wait_send()
        hop(vx2, vx2, 1, seq).wait_send()


def unsort_kernel(o_ref, out_hbm, stage, sems):
    rows = iota((BLK, BLK), 0)
    perm = (iota((BLK, BLK), 1) == ((rows & 15) << 4) + (rows >> 4)).astype(jnp.bfloat16)
    copies = []
    for j in range(0, NB, 2):
        cols = []
        for h in (j, j + 1):
            groups = [SHIFTS.index((r - h) % 16) for r in range(16)]
            cols.append(
                jnp.concatenate([o_ref[h, g * 16 : (g + 1) * 16] for g in groups], axis=0)
            )
        stage[:, j * HD : (j + 2) * HD] = jnp.dot(
            perm, jnp.concatenate(cols, axis=1), preferred_element_type=jnp.float32
        ).astype(jnp.bfloat16)
        if j % 4 == 2:
            here = (slice(None), pl.ds((j - 2) * HD, 4 * HD))
            copy = pltpu.make_async_copy(stage.at[here], out_hbm.at[here], sems.at[j // 4])
            copy.start()
            copies.append(copy)
    for copy in copies:
        copy.wait()


def shards(queries, keys, values):
    bf, f32 = jnp.bfloat16, jnp.float32
    vm = pltpu.VMEM
    blocks = vm((NB, BLK, HD), bf)
    dma = pltpu.SemaphoreType.DMA
    nk = len(K_PARTS)
    queries, keys, values = (
        pltpu.with_memory_space_constraint(x, pltpu.HBM) for x in (queries, keys, values)
    )
    sorted_out = pl.pallas_call(
        kernel,
        out_shape=pltpu.VMEM((NB, BLK, HD), bf),
        in_specs=[pl.BlockSpec(memory_space=pltpu.HBM)] * 3,
        out_specs=pl.BlockSpec(memory_space=pltpu.VMEM),
        scratch_shapes=[
            vm((2, BLK, NB * HD), bf),
            *[blocks] * 7,
            vm((NB, 64, HD), bf), vm((NB, 64, HD), bf),
            vm((2, NB, 32, HD), bf), vm((2, NB, 32, HD), bf),
            vm((2, 2, NB, 16, HD), bf), vm((2, 2, NB, 16, HD), bf),
            *[vm((2, NB, CH, HD), f32)] * 3,
            vm((BLK, BLK), bf), vm((BLK, BLK), bf), vm((BLK, BLK), f32),
            vm((128, 128), f32), vm((64, 128), f32), vm((64, 128), f32), vm((32, 128), f32),
            dma((2,)), dma, dma((NCH,)), dma((nk,)), dma, dma((NCH,)),
            dma((NCH,)), dma((nk,)), dma, dma((NCH,)), dma((10,)), dma((10,)),
        ],
        compiler_params=pltpu.CompilerParams(
            collective_id=0, has_side_effects=True, vmem_limit_bytes=48 * 2**20
        ),
    )(queries, keys, values)
    sorted_out = pltpu.with_memory_space_constraint(sorted_out, pltpu.VMEM)
    return pl.pallas_call(
        unsort_kernel,
        out_shape=jax.ShapeDtypeStruct((BLK, NB * HD), bf),
        in_specs=[pl.BlockSpec(memory_space=pltpu.VMEM)],
        out_specs=pl.BlockSpec(memory_space=pl.ANY),
        scratch_shapes=[vm((BLK, NB * HD), bf), dma((4,))],
        compiler_params=pltpu.CompilerParams(vmem_limit_bytes=16 * 2**20),
    )(sorted_out)


def solution(mesh):
    spec = P(("seq", "head"), None)
    return jax.shard_map(
        shards, mesh=mesh, in_specs=(spec, spec, spec), out_specs=spec, check_vma=False
    )
```

time: 65.4 us -> 57.6 us (0.88)
  Pallas kernels: 62.7 us -> 57.3 us
  local copies, waits for them, and re-layouts: 2.3 us -> 0 us
    pallas_call x1 -> x2, Pallas kernels: 62.7 us -> 57.3 us  [the longest x1 56 us: shards(): pl.pallas_call(kernel, out_shape=pltpu.VMEM((NB, BLK, HD), bf), in_specs=...]
    unnamed x1 -> x0, local copies, waits for them, and re-layouts: 2.3 us -> none
where the time goes in v2:
time: 57.6 us; the launch traced here: 57.4 us
  Pallas kernels  57.3 us (99%)
    pallas_call x1, Pallas kernels, shards(): pl.pallas_call(kernel, out_shape=pltpu.VMEM((NB, BLK, HD), bf), in_specs=...  56 us
    pallas_call x1, Pallas kernels, shards(): pl.pallas_call(unsort_kernel, out_shape=jax.ShapeDtypeStruct((BLK, NB * H...  1.23 us

profile of v2, /device:TPU:0, one launch (start us, length us, event | category | flops | bytes accessed | tf_op | source)
XLA Modules:
  0.0 57.4 jit_solution(16671240479156478370)
XLA Ops:
  0.0 56.0 %shard_map.37.o_ref = bf16[16,256,128]{2,1,0:T(8,128)(2,1)S(1)} custom-call(bf16[256,2048]{1,0:T(8,128)(2,1)} %q_hbm.1, bf16[256,2048]{1,0:T(8,128)(2,1)} %k_hbm.1, bf16[256,2048]{1,0:T(8,128)(2,1)} %v_hbm.1), custom_call_target="tpu_custom_call" | custom-call | tf_op jit(solution)/shard_map/pallas_call | solution.py:421
  56.0 1.2 %shard_map.38 = bf16[256,2048]{1,0:T(8,128)(2,1)} custom-call(bf16[16,256,128]{2,1,0:T(8,128)(2,1)S(1)} %shard_map.37.o_ref), custom_call_target="tpu_custom_call" | custom-call | tf_op jit(solution)/shard_map/pallas_call | solution.py:443

commit v3 on v2

--- a/solution.py
+++ b/solution.py
@@ -72,24 +72,21 @@
     flip = 1 + 2 * (seq % 2)
     peers = [((z + dz * flip) % 4) * 4 + (y + dy * flip) % 4 for dz, dy in ORDER]
 
+    barrier = pltpu.get_barrier_semaphore()
+    for p in peers:
+        pl.semaphore_signal(barrier, inc=1, device_id=(seq, p), device_id_type=MESH)
+    core = seq % 2
+    partner = seq + 1 - 2 * core
+    other_half = (seq // 4 + 1) % 2 * 4 + core
+    beside = seq + 2 - 4 * (seq // 2 % 2)
+    for t in (partner, beside, other_half, other_half + 2):
+        pl.semaphore_signal(barrier, inc=1, device_id=(t, me), device_id_type=MESH)
+
     loads = []
     for i, src in enumerate((k_hbm, q_hbm)):
         cp = pltpu.make_async_copy(src, x_in.at[i], in_sem.at[i])
         cp.start()
         loads.append(cp)
-
-    barrier = pltpu.get_barrier_semaphore()
-    for p in peers:
-        pl.semaphore_signal(barrier, inc=1, device_id=(seq, p), device_id_type=MESH)
-    for d in range(1, 8):
-        pl.semaphore_signal(
-            barrier, inc=1, device_id=((seq + d) % 8, me), device_id_type=MESH
-        )
-
-    rows = iota((BLK, BLK), 0)
-    perm_ref[...] = (iota((BLK, BLK), 1) == ((rows & 15) << 4) + (rows >> 4)).astype(
-        jnp.bfloat16
-    )
 
     def sort_rows(i, dst):
         for j in range(0, NB, 2):
@@ -119,6 +116,23 @@
             if i < len(between):
                 between[i]()
 
+    def send_by_row(src, dst, ssem, rsem, part, idx, passes):
+        lo, hi = part
+        rows = pl.ds(lo, hi - lo)
+        for first, last in passes:
+            for p in peers:
+
+                @pl.when((p >= 4 * first) & (p < 4 * last))
+                def _(p=p):
+                    pltpu.make_async_remote_copy(
+                        src_ref=src.at[p, rows],
+                        dst_ref=dst.at[me, rows],
+                        send_sem=ssem.at[idx],
+                        recv_sem=rsem.at[idx],
+                        device_id=(seq, p),
+                        device_id_type=MESH,
+                    ).start()
+
     def wait_all(buf, sem, part, idx):
         lo, hi = part
         view = buf.at[pl.ds(0, NB - 1), pl.ds(lo, hi - lo)]
@@ -129,7 +143,7 @@
 
     own = pltpu.make_async_copy(head_cols(v_hbm, me), v_raw.at[me], own_sem)
     own.start()
-    pl.semaphore_wait(barrier, NB - 1 + 7)
+    pl.semaphore_wait(barrier, NB - 1 + 4)
     for p in peers:
         pltpu.make_async_remote_copy(
             src_ref=head_cols(v_hbm, p),
@@ -139,6 +153,11 @@
             device_id=(seq, p),
             device_id_type=MESH,
         ).start()
+    rows = iota((BLK, BLK), 0)
+    perm_ref[...] = (iota((BLK, BLK), 1) == ((rows & 15) << 4) + (rows >> 4)).astype(
+        jnp.bfloat16
+    )
+
     loads[0].wait()
     sort_rows(0, k_send)
     send(k_send, k_recv, k_ss, k_rs, K_PARTS[0], 0)
@@ -192,8 +211,6 @@
         hop(k_recv.at[:, pl.ds(0, 64)], kx2, 0, (seq // 2) * 2 + 1).start()
         hop(v_recv.at[:, pl.ds(0, 64)], vx2, 1, (seq // 2) * 2 + 1).start()
 
-    core = seq % 2
-    partner = seq + 1 - 2 * core
     near_chip = seq % 4 < 2
     far_chip = seq < 4
 
@@ -345,7 +362,10 @@
             total = jnp.sum(l_ref[state, b], axis=1, keepdims=True)
             o_send[b, pl.ds(lo, CH)] = (acc_ref[state, b] / total).astype(jnp.bfloat16)
         o_recv[me, pl.ds(lo, CH)] = o_send[me, pl.ds(lo, CH)]
-        send(o_send, o_recv, o_ss, o_rs, Q_PARTS[chunk], chunk)
+        if True:
+            send_by_row(o_send, o_recv, o_ss, o_rs, Q_PARTS[chunk], chunk, [(0, 2), (2, 4)])
+        else:
+            send(o_send, o_recv, o_ss, o_rs, Q_PARTS[chunk], chunk)
 
     own_rows(0)
     for chunk in range(1, NCH):

time: 57.6 us -> 57.1 us (level)
  no operation moved by 1% of the time
where the time goes in v3:
time: 57.1 us; the launch traced here: 57 us
  Pallas kernels  56.8 us (99%)
    pallas_call x1, Pallas kernels, shards(): pl.pallas_call(kernel, out_shape=pltpu.VMEM((NB, BLK, HD), bf), in_specs=...  55.6 us
    pallas_call x1, Pallas kernels, shards(): pl.pallas_call(unsort_kernel, out_shape=jax.ShapeDtypeStruct((BLK, NB * H...  1.23 us

profile of v3, /device:TPU:0, one launch (start us, length us, event | category | flops | bytes accessed | tf_op | source)
XLA Modules:
  0.0 57.0 jit_solution(10998728767113750456)
XLA Ops:
  0.0 55.6 %shard_map.37.o_ref = bf16[16,256,128]{2,1,0:T(8,128)(2,1)S(1)} custom-call(bf16[256,2048]{1,0:T(8,128)(2,1)} %q_hbm.1, bf16[256,2048]{1,0:T(8,128)(2,1)} %k_hbm.1, bf16[256,2048]{1,0:T(8,128)(2,1)} %v_hbm.1), custom_call_target="tpu_custom_call" | custom-call | tf_op jit(solution)/shard_map/pallas_call | solution.py:441
  55.6 1.2 %shard_map.38 = bf16[256,2048]{1,0:T(8,128)(2,1)} custom-call(bf16[16,256,128]{2,1,0:T(8,128)(2,1)S(1)} %shard_map.37.o_ref), custom_call_target="tpu_custom_call" | custom-call | tf_op jit(solution)/shard_map/pallas_call | solution.py:463

commit v4 on v3

--- a/solution.py
+++ b/solution.py
@@ -13,6 +13,7 @@
 NB = 16
 CH = 64
 NCH = BLK // CH
+SPLIT = (1, 2, 3)
 FAR_AFTER = 2
 SCALE = HD**-0.5 * math.log2(math.e)
 LOW = -1e30
@@ -206,11 +207,6 @@
             device_id_type=MESH,
         )
 
-    @pl.when(seq % 2 == 0)
-    def _():
-        hop(k_recv.at[:, pl.ds(0, 64)], kx2, 0, (seq // 2) * 2 + 1).start()
-        hop(v_recv.at[:, pl.ds(0, 64)], vx2, 1, (seq // 2) * 2 + 1).start()
-
     near_chip = seq % 4 < 2
     far_chip = seq < 4
 
@@ -224,6 +220,11 @@
         def _():
             target = 4 + 2 * step + core
             hop(src.at[:, pl.ds(0, 16)], dst.at[core, seq // 2 % 2], idx, target).start()
+
+    def hop2(src, dst, idx):
+        @pl.when(core == 0)
+        def _():
+            hop(src.at[:, pl.ds(0, 64)], dst, idx, partner).start()
 
     hops = [functools.partial(hop3, *x) for x in ((k_recv, kx3, 2), (v_recv, vx3, 3))]
     hops += [
@@ -231,6 +232,7 @@
         for step in range(2)
         for x in ((k_recv, kx4, 4), (v_recv, vx4, 5))
     ]
+    hops += [functools.partial(hop2, *x) for x in ((k_recv, kx2, 0), (v_recv, vx2, 1))]
     send(q_send, q_recv, q_ss, q_rs, Q_PARTS[1], 1, between=hops)
     for i in range(2, NCH):
         send(q_send, q_recv, q_ss, q_rs, Q_PARTS[i], i)
@@ -330,7 +332,7 @@
 
     wait_all(k_recv, k_rs, K_PARTS[1], 1)
 
-    def own_rows(chunk):
+    def own_rows(chunk, between=None):
         lo = chunk * CH
         nested = lo < 128
 
@@ -346,6 +348,8 @@
             return carry
 
         segment(0, 0)
+        if between is not None:
+            between()
         segment(1, 0)
         if nested:
             cross(
@@ -355,23 +359,29 @@
                 mult1[...] if chunk == 0 else None,
             )
 
-    def finish(chunk):
+    def finish(chunk, first=0, last=4):
         lo = chunk * CH
         state = min(chunk, 1)
-        for b in range(NB):
+        for b in range(4 * first, 4 * last):
             total = jnp.sum(l_ref[state, b], axis=1, keepdims=True)
             o_send[b, pl.ds(lo, CH)] = (acc_ref[state, b] / total).astype(jnp.bfloat16)
-        o_recv[me, pl.ds(lo, CH)] = o_send[me, pl.ds(lo, CH)]
-        if True:
-            send_by_row(o_send, o_recv, o_ss, o_rs, Q_PARTS[chunk], chunk, [(0, 2), (2, 4)])
-        else:
-            send(o_send, o_recv, o_ss, o_rs, Q_PARTS[chunk], chunk)
+
+        @pl.when((me >= 4 * first) & (me < 4 * last))
+        def _():
+            o_recv[me, pl.ds(lo, CH)] = o_send[me, pl.ds(lo, CH)]
+
+        passes = [(i, i + 2) for i in range(first, last, 2)]
+        send_by_row(o_send, o_recv, o_ss, o_rs, Q_PARTS[chunk], chunk, passes)
 
     own_rows(0)
     for chunk in range(1, NCH):
         wait_all(q_recv, q_rs, Q_PARTS[chunk], chunk)
-        own_rows(chunk)
-        finish(chunk)
+        if chunk in SPLIT:
+            own_rows(chunk, functools.partial(finish, chunk, 0, 2))
+            finish(chunk, 2, 4)
+        else:
+            own_rows(chunk)
+            finish(chunk)
         if chunk == 1:
             hand_over()
         if chunk == FAR_AFTER:

time: 57.1 us -> 56.8 us (level)
  no operation moved by 1% of the time
where the time goes in v4:
time: 56.8 us; the launch traced here: 56.5 us
  Pallas kernels  56.3 us (99%)
    pallas_call x1, Pallas kernels, shards(): pl.pallas_call(kernel, out_shape=pltpu.VMEM((NB, BLK, HD), bf), in_specs=...  55.1 us
    pallas_call x1, Pallas kernels, shards(): pl.pallas_call(unsort_kernel, out_shape=jax.ShapeDtypeStruct((BLK, NB * H...  1.23 us

profile of v4, /device:TPU:0, one launch (start us, length us, event | category | flops | bytes accessed | tf_op | source)
XLA Modules:
  0.0 56.5 jit_solution(8919903489844269664)
XLA Ops:
  0.0 55.1 %shard_map.37.o_ref = bf16[16,256,128]{2,1,0:T(8,128)(2,1)S(1)} custom-call(bf16[256,2048]{1,0:T(8,128)(2,1)} %q_hbm.1, bf16[256,2048]{1,0:T(8,128)(2,1)} %k_hbm.1, bf16[256,2048]{1,0:T(8,128)(2,1)} %v_hbm.1), custom_call_target="tpu_custom_call" | custom-call | tf_op jit(solution)/shard_map/pallas_call | solution.py:451
  55.1 1.2 %shard_map.38 = bf16[256,2048]{1,0:T(8,128)(2,1)} custom-call(bf16[16,256,128]{2,1,0:T(8,128)(2,1)S(1)} %shard_map.37.o_ref), custom_call_target="tpu_custom_call" | custom-call | tf_op jit(solution)/shard_map/pallas_call | solution.py:473

commit v5 on v4

--- a/solution.py
+++ b/solution.py
@@ -86,8 +86,8 @@
     loads = []
     for i, src in enumerate((k_hbm, q_hbm)):
         cp = pltpu.make_async_copy(src, x_in.at[i], in_sem.at[i])
-        cp.start()
         loads.append(cp)
+    loads[0].start()
 
     def sort_rows(i, dst):
         for j in range(0, NB, 2):
@@ -154,6 +154,8 @@
             device_id=(seq, p),
             device_id_type=MESH,
         ).start()
+    loads[1].start()
+
     rows = iota((BLK, BLK), 0)
     perm_ref[...] = (iota((BLK, BLK), 1) == ((rows & 15) << 4) + (rows >> 4)).astype(
         jnp.bfloat16

time: 56.8 us -> 56.8 us (level)
  no operation moved by 1% of the time
where the time goes in v5:
time: 56.8 us; the launch traced here: 56.5 us
  Pallas kernels  56.3 us (99%)
    pallas_call x1, Pallas kernels, shards(): pl.pallas_call(kernel, out_shape=pltpu.VMEM((NB, BLK, HD), bf), in_specs=...  55.1 us
    pallas_call x1, Pallas kernels, shards(): pl.pallas_call(unsort_kernel, out_shape=jax.ShapeDtypeStruct((BLK, NB * H...  1.23 us

profile of v5, /device:TPU:0, one launch (start us, length us, event | category | flops | bytes accessed | tf_op | source)
XLA Modules:
  0.0 56.5 jit_solution(15254844485648027414)
XLA Ops:
  0.0 55.1 %shard_map.37.o_ref = bf16[16,256,128]{2,1,0:T(8,128)(2,1)S(1)} custom-call(bf16[256,2048]{1,0:T(8,128)(2,1)} %q_hbm.1, bf16[256,2048]{1,0:T(8,128)(2,1)} %k_hbm.1, bf16[256,2048]{1,0:T(8,128)(2,1)} %v_hbm.1), custom_call_target="tpu_custom_call" | custom-call | tf_op jit(solution)/shard_map/pallas_call | solution.py:453
  55.1 1.2 %shard_map.38 = bf16[256,2048]{1,0:T(8,128)(2,1)} custom-call(bf16[16,256,128]{2,1,0:T(8,128)(2,1)S(1)} %shard_map.37.o_ref), custom_call_target="tpu_custom_call" | custom-call | tf_op jit(solution)/shard_map/pallas_call | solution.py:475
